TPU v7x, 32 devices: a whole 2x2x4 slice. The times are simulated.
32 devices in a mesh: dp: 16 (over z, y, x), tensor: 2 (over core).
Axes of the slice: x: 2, y: 2, z: 4, core: 2. Of those that a mesh axis runs over, the one named last changes fastest.
Arguments:
- inputs: bfloat16 [2, 8192, 1024], P(None, ('dp', 'tensor')), may hold values from -6 to 6
- lengths: int32 [2, 16, 8], P(None, 'dp'), may hold values from 0 to 512, as said below
- query_weight: bfloat16 [1024, 1024], P(None, 'tensor'), may hold values from -0.1875 to 0.1875
- key_weight: bfloat16 [1024, 1024], P(None, 'tensor'), may hold values from -0.1875 to 0.1875
- value_weight: bfloat16 [1024, 1024], P(None, 'tensor'), may hold values from -0.1875 to 0.1875
- output_weight: bfloat16 [1024, 1024], P('tensor'), may hold values from -0.1875 to 0.1875
- inner_weight: bfloat16 [1024, 4096], P(None, 'tensor'), may hold values from -0.1875 to 0.1875
- outer_weight: bfloat16 [4096, 1024], P('tensor'), may hold values from -0.09375 to 0.09375
- entry_gain: float32 [1024], replicated, may hold values from 0.25 to 1.75
- entry_bias: float32 [1024], replicated, may hold values from -3 to 3
- merge_gain: float32 [1024], replicated, may hold values from 0.25 to 1.75
- merge_bias: float32 [1024], replicated, may hold values from -3 to 3
- inlet_gain: float32 [1024], replicated, may hold values from 0.25 to 1.75
- inlet_bias: float32 [1024], replicated, may hold values from -3 to 3
- outlet_gain: float32 [1024], replicated, may hold values from 0.25 to 1.75
- outlet_bias: float32 [1024], replicated, may hold values from -3 to 3
- cotangent: bfloat16 [2, 8192, 1024], P(None, ('dp', 'tensor')), may hold values from -6 to 6
Outputs:
- outputs: bfloat16 [2, 8192, 1024], P(None, ('dp', 'tensor'))
- input_grad: bfloat16 [2, 8192, 1024], P(None, ('dp', 'tensor'))
- query_grad: float32 [1024, 1024], P(None, 'tensor')
- key_grad: float32 [1024, 1024], P(None, 'tensor')
- value_grad: float32 [1024, 1024], P(None, 'tensor')
- output_grad: float32 [1024, 1024], P('tensor')
- inner_grad: float32 [1024, 4096], P(None, 'tensor')
- outer_grad: float32 [4096, 1024], P('tensor')
- gain_entry: float32 [1024], replicated
- bias_entry: float32 [1024], replicated
- gain_merge: float32 [1024], replicated
- bias_merge: float32 [1024], replicated
- gain_inlet: float32 [1024], replicated
- bias_inlet: float32 [1024], replicated
- gain_outlet: float32 [1024], replicated
- bias_outlet: float32 [1024], replicated
Inputs may be any that keep to these rules, and one draw needn't show every extreme that they name: `lengths`: each row lists the 8 sequences of one buffer packed in order from its first row; they sum to at most 512, the rest of the buffer is padding; slots may be empty; some buffer holds a single sequence of exactly 512.
All inputs are finite; a program needn't handle non-finite values.
Results may differ from a plain program's by a relative error of at most 0.015.
The roundings to bfloat16 on the way count: a program that leaves them out, or rounds other values in their place, can miss the bound.
Values may be sent and summed in bfloat16 or wider, within the bound.
No kernel may reach another device: no remote copies, remote signals or barrier semaphores. Data moves between devices by JAX's collectives and lax.ppermute only.
A program may use at most 192 MiB of HBM per device.

v0:
```python
import math

import jax
import jax.numpy as jnp
from jax import lax
from jax.sharding import PartitionSpec as P

HEAD = 64


NEGATIVE = -1e30


def layer_norm(values, gain, bias):
    center = values - jnp.mean(values, axis=-1, keepdims=True)
    spread = jnp.mean(center * center, axis=-1, keepdims=True)
    return center * lax.rsqrt(spread + 1e-05) * gain + bias


def exact_gelu(values):
    return jax.nn.gelu(values, approximate=False)


def seq_layout(lens, rows):
    ends = jnp.cumsum(lens, dtype=jnp.int32)
    index = jnp.arange(rows, dtype=jnp.int32)
    after = index[:, None] >= ends[None, :]
    segment = jnp.sum(after.astype(jnp.int32), axis=1)
    begin = jnp.max(jnp.where(after, ends[None, :], 0), axis=1)
    return (segment, (index - begin).astype(jnp.float32))


def rotary_tables(place, width):
    half = width // 2
    rate = jnp.exp(jnp.arange(half, dtype=jnp.float32) * (-math.log(10000.0) / half))
    angle = place[:, None] * rate[None, :]
    return (jnp.cos(angle)[:, None, :], jnp.sin(angle)[:, None, :])


def rotate(values, cosine, sine):
    half = values.shape[-1] // 2
    first = values[..., :half]
    second = values[..., half:]
    return jnp.concatenate(
        [first * cosine - second * sine, first * sine + second * cosine], axis=-1
    )


def rotate_back(grads, cosine, sine):
    half = grads.shape[-1] // 2
    first = grads[..., :half]
    second = grads[..., half:]
    return jnp.concatenate(
        [first * cosine + second * sine, second * cosine - first * sine], axis=-1
    )


def contract_rows(left, right):
    return lax.dot_general(
        left, right, (((0,), (0,)), ((), ())), preferred_element_type=jnp.float32
    )


def times_transpose(left, right):
    return lax.dot_general(
        left, right, (((1,), (1,)), ((), ())), preferred_element_type=jnp.float32
    )


def masked_scores(query_block, keys, segment, begin, block):
    rows = keys.shape[0]
    scores = (
        jnp.einsum("qhd,khd->hqk", query_block, keys, preferred_element_type=jnp.float32) * 0.125
    )
    query_index = begin + jnp.arange(block, dtype=jnp.int32)
    key_index = jnp.arange(rows, dtype=jnp.int32)
    allowed = (segment[:, None] == segment[None, :]) & (key_index[None, :] <= query_index[:, None])
    return jnp.where(allowed[None], scores, NEGATIVE)


def attend_forward(query, keys, values, segment, block):
    rows = keys.shape[0]

    def one_block(number):
        begin = number * block
        scores = masked_scores(query, keys, segment, begin, block)
        peak = jnp.max(scores, axis=-1, keepdims=True)
        raised = jnp.exp(scores - peak)
        total = jnp.sum(raised, axis=-1, keepdims=True)
        probs = (raised / total).astype(jnp.bfloat16)
        attended = jnp.einsum("hqk,khd->qhd", probs, values, preferred_element_type=jnp.float32)
        return (attended, (peak + jnp.log(total))[..., 0])

    attended, logsum = lax.map(one_block, jnp.arange(rows // block, dtype=jnp.int32))
    return (attended.reshape(rows, query.shape[1], query.shape[2]), logsum)


def attend_backward(query, keys, values, mixed_grad, segment, logsum, block):
    rows = keys.shape[0]

    def one_block(carry, packed):
        keys_acc, values_acc = carry
        number, block_logsum = packed
        begin = number * block
        scores = masked_scores(query, keys, segment, begin, block)
        probs = jnp.exp(scores - block_logsum[..., None])
        prob_grad = jnp.einsum(
            "qhd,khd->hqk", mixed_grad, values, preferred_element_type=jnp.float32
        )
        offset = jnp.sum(probs * prob_grad, axis=-1, keepdims=True)
        score_grad = (probs * (prob_grad - offset)).astype(jnp.bfloat16)
        query_part = (
            jnp.einsum("hqk,khd->qhd", score_grad, keys, preferred_element_type=jnp.float32) * 0.125
        )
        keys_acc = (
            keys_acc
            + jnp.einsum("hqk,qhd->khd", score_grad, query, preferred_element_type=jnp.float32)
            * 0.125
        )
        values_acc = values_acc + jnp.einsum(
            "hqk,qhd->khd",
            probs.astype(jnp.bfloat16),
            mixed_grad,
            preferred_element_type=jnp.float32,
        )
        return ((keys_acc, values_acc), query_part)

    empty = jnp.zeros(keys.shape, jnp.float32)
    numbers = jnp.arange(rows // block, dtype=jnp.int32)
    (keys_grad, values_grad), query_grad = lax.scan(one_block, (empty, empty), (numbers, logsum))
    return (query_grad.reshape(keys.shape), keys_grad, values_grad)


def on_device(
    inputs,
    lengths,
    query_weight,
    key_weight,
    value_weight,
    output_weight,
    inner_weight,
    outer_weight,
    entry_gain,
    entry_bias,
    merge_gain,
    merge_bias,
    inlet_gain,
    inlet_bias,
    outlet_gain,
    outlet_bias,
    cotangent,
):
    groups = lax.axis_size("tensor")
    local_rows = inputs.shape[1]
    rows = local_rows * groups
    width = query_weight.shape[1]
    block = min(512, rows)
    joined = jnp.concatenate([query_weight, key_weight, value_weight], axis=1)
    inner_use, outer_use = (inner_weight, outer_weight)
    joined_acc = jnp.zeros(joined.shape, jnp.float32)
    output_acc = jnp.zeros(output_weight.shape, jnp.float32)
    inner_acc = jnp.zeros(inner_use.shape, jnp.float32)
    outer_acc = jnp.zeros(outer_use.shape, jnp.float32)
    norm_acc = [jnp.zeros(entry_gain.shape, jnp.float32) for index in range(8)]
    result_list = []
    grad_list = []
    for micro in range(inputs.shape[0]):
        segment, place = seq_layout(lengths[micro, 0], rows)
        cosine, sine = rotary_tables(place, HEAD)
        resid = inputs[micro].astype(jnp.float32)
        normed, entry_pull = jax.vjp(layer_norm, resid, entry_gain, entry_bias)
        gathered = lax.all_gather(normed.astype(jnp.bfloat16), "tensor", axis=0, tiled=True)
        projected = jnp.dot(gathered, joined, preferred_element_type=jnp.float32)
        query = rotate(
            projected[:, :width].reshape(rows, width // HEAD, HEAD), cosine, sine
        ).astype(jnp.bfloat16)
        keys = rotate(
            projected[:, width : 2 * width].reshape(rows, width // HEAD, HEAD), cosine, sine
        ).astype(jnp.bfloat16)
        values = projected[:, 2 * width :].reshape(rows, width // HEAD, HEAD).astype(jnp.bfloat16)
        attended, logsum = attend_forward(query, keys, values, segment, block)
        mixed = attended.reshape(rows, width).astype(jnp.bfloat16)
        branch = lax.psum_scatter(
            jnp.dot(mixed, output_weight, preferred_element_type=jnp.float32),
            "tensor",
            scatter_dimension=0,
            tiled=True,
        )
        merged, merge_pull = jax.vjp(layer_norm, branch, merge_gain, merge_bias)
        hidden = resid + merged
        inlet, inlet_pull = jax.vjp(layer_norm, hidden, inlet_gain, inlet_bias)
        inlet_low = inlet.astype(jnp.bfloat16)
        feed = lax.all_gather(inlet_low, "tensor", axis=0, tiled=True)
        pre_act = jnp.dot(feed, inner_use, preferred_element_type=jnp.float32)
        activated, gelu_pull = jax.vjp(exact_gelu, pre_act)
        act_low = activated.astype(jnp.bfloat16)
        second = lax.psum_scatter(
            jnp.dot(act_low, outer_use, preferred_element_type=jnp.float32),
            "tensor",
            scatter_dimension=0,
            tiled=True,
        )
        finished, outlet_pull = jax.vjp(layer_norm, second, outlet_gain, outlet_bias)
        result_list.append((hidden + finished).astype(jnp.bfloat16))
        upstream = cotangent[micro].astype(jnp.float32)
        second_grad, outlet_gain_part, outlet_bias_part = outlet_pull(upstream)
        second_low = second_grad.astype(jnp.bfloat16)
        back_feed = lax.all_gather(second_low, "tensor", axis=0, tiled=True)
        outer_term = contract_rows(act_low, back_feed)
        act_grad = times_transpose(back_feed, outer_use)
        (pre_grad,) = gelu_pull(act_grad)
        pre_low = pre_grad.astype(jnp.bfloat16)
        inner_term = contract_rows(feed, pre_low)
        inlet_grad = lax.psum_scatter(
            times_transpose(pre_low, inner_use), "tensor", scatter_dimension=0, tiled=True
        )
        hidden_part, inlet_gain_part, inlet_bias_part = inlet_pull(inlet_grad)
        hidden_grad = upstream + hidden_part
        branch_grad, merge_gain_part, merge_bias_part = merge_pull(hidden_grad)
        back_mix = lax.all_gather(branch_grad.astype(jnp.bfloat16), "tensor", axis=0, tiled=True)
        output_term = contract_rows(mixed, back_mix)
        mixed_grad = (
            times_transpose(back_mix, output_weight)
            .astype(jnp.bfloat16)
            .reshape(rows, width // HEAD, HEAD)
        )
        query_part, keys_part, values_part = attend_backward(
            query, keys, values, mixed_grad, segment, logsum, block
        )
        projected_grad = jnp.concatenate(
            [
                rotate_back(query_part, cosine, sine).reshape(rows, width),
                rotate_back(keys_part, cosine, sine).reshape(rows, width),
                values_part.reshape(rows, width),
            ],
            axis=1,
        ).astype(jnp.bfloat16)
        joined_term = contract_rows(gathered, projected_grad)
        normed_grad = lax.psum_scatter(
            times_transpose(projected_grad, joined).astype(jnp.bfloat16),
            "tensor",
            scatter_dimension=0,
            tiled=True,
        ).astype(jnp.float32)
        resid_part, entry_gain_part, entry_bias_part = entry_pull(normed_grad)
        grad_list.append((hidden_grad + resid_part).astype(jnp.bfloat16))
        parts = [
            entry_gain_part,
            entry_bias_part,
            merge_gain_part,
            merge_bias_part,
            inlet_gain_part,
            inlet_bias_part,
            outlet_gain_part,
            outlet_bias_part,
        ]
        norm_acc = [total + piece for total, piece in zip(norm_acc, parts)]
        joined_acc = joined_acc + joined_term
        output_acc = output_acc + output_term
        inner_acc = inner_acc + inner_term
        outer_acc = outer_acc + outer_term
    joined_acc, output_acc, inner_acc, outer_acc = lax.psum(
        (joined_acc, output_acc, inner_acc, outer_acc), "dp"
    )
    norm_sums = lax.psum(
        (
            norm_acc[0],
            norm_acc[1],
            norm_acc[2],
            norm_acc[3],
            norm_acc[4],
            norm_acc[5],
            norm_acc[6],
            norm_acc[7],
        ),
        ("dp", "tensor"),
    )
    return (
        jnp.stack(result_list),
        jnp.stack(grad_list),
        joined_acc[:, :width],
        joined_acc[:, width : 2 * width],
        joined_acc[:, 2 * width :],
        output_acc,
        inner_acc,
        outer_acc,
        norm_sums[0],
        norm_sums[1],
        norm_sums[2],
        norm_sums[3],
        norm_sums[4],
        norm_sums[5],
        norm_sums[6],
        norm_sums[7],
    )


def solution(mesh):
    placed = (
        P(None, ("dp", "tensor"), None),
        P(None, "dp", None),
        P(None, "tensor"),
        P(None, "tensor"),
        P(None, "tensor"),
        P("tensor", None),
        P(None, "tensor"),
        P("tensor", None),
        P(),
        P(),
        P(),
        P(),
        P(),
        P(),
        P(),
        P(),
        P(None, ("dp", "tensor"), None),
    )
    return jax.shard_map(
        on_device,
        mesh=mesh,
        in_specs=placed,
        out_specs=(
            P(None, ("dp", "tensor"), None),
            P(None, ("dp", "tensor"), None),
            P(None, "tensor"),
            P(None, "tensor"),
            P(None, "tensor"),
            P("tensor", None),
            P(None, "tensor"),
            P("tensor", None),
            P(),
            P(),
            P(),
            P(),
            P(),
            P(),
            P(),
            P(),
        ),
        check_vma=False,
    )
```

profile of v0, /device:TPU:0, one launch (start us, length us, event | category | flops | bytes accessed | tf_op | source)
XLA Modules:
  0.0 979.6 jit_solution(8197130521890826717)
XLA Ops:
  21.8 3.9 all-gather.13.cloned.1.call-done
  25.8 4.0 fusion.125
  47.3 4.0 fusion.122
  70.1 8.1 reduce-scatter.9.cloned.1.call-done
  86.6 9.5 all-gather.15.cloned.1.call-done
  96.1 15.0 %multiply_convert_fusion.2 = (bf16[512,2048]{1,0:T(8,128)(2,1)S(1)}, f32[512,2048]{1,0:T(8,128)}, f32[512,2048]{1,0:T(8,128)}) fusion(bf16[512,1024]{1,0:T(8,128)(2,1)} %all-gather.15.cloned.1.call-done, bf16[1024,2048]{1,0:T(8,128)(2,1)} %param.23), kind=kOutput, calls=%fused_computation.27 | convolution fusion | flops 2215641088 | bytes 15728640 | tf_op jit(solution)/shard_map/dot_general | solution.py:194
  116.6 14.9 %multiply_convert_fusion.3 = (bf16[512,2048]{1,0:T(8,128)(2,1)S(1)}, f32[512,2048]{1,0:T(8,128)}, f32[512,2048]{1,0:T(8,128)}) fusion(bf16[512,1024]{1,0:T(8,128)(2,1)} %all-gather.11.cloned.1.call-done, bf16[1024,2048]{1,0:T(8,128)(2,1)} %param.23), kind=kOutput, calls=%fused_computation.40 | convolution fusion | flops 2215641088 | bytes 15728640 | tf_op jit(solution)/shard_map/dot_general | solution.py:194
  139.5 7.9 reduce-scatter.11.cloned.1.call-done
  158.7 7.9 all-gather.21.cloned.1.call-done
  166.6 8.5 add_convert_fusion
  180.3 8.5 add_convert_fusion.1
  190.2 3.7 fusion.128
  194.2 7.5 fusion.132
  201.7 4.4 reduce-scatter.17.cloned.1.call-done
  214.1 9.5 convolution_add_fusion.1
  223.7 5.7 fusion.131
  232.9 5.4 multiply_reduce_fusion
  251.6 5.4 multiply_reduce_fusion.1
  268.4 9.9 %convolution_add_fusion.2 = f32[1024,2048]{1,0:T(8,128)} fusion(f32[1024,2048]{1,0:T(8,128)} %fusion.131, bf16[512,1024]{1,0:T(8,128)(2,1)S(1)} %copy-done.22, bf16[512,2048]{1,0:T(8,128)(2,1)} %copy-done.23), kind=kOutput, calls=%fused_computation.58 | convolution fusion | flops 2149580800 | bytes 19922944 | tf_op jit(solution)/shard_map/dot_general | solution.py:59
  283.6 4.6 convolution_add_fusion
  296.6 45.4 %all-reduce = (f32[1024]{0:T(1024)}, f32[1024]{0:T(1024)}, f32[1024]{0:T(1024)}, f32[1024]{0:T(1024)}, f32[1024]{0:T(1024)}, /*index=5*/f32[1024]{0:T(1024)}, f32[1024]{0:T(1024)}, f32[1024]{0:T(1024)}) all-reduce(f32[1024]{0:T(1024)S(1)} %add.355, f32[1024]{0:T(1024)S(1)} %add.356, ...), channel_id=1, replica_groups=mesh['dp'=16,'tensor'=2] {'dp','tensor'}, use_global_device_ids=true, to_apply=%region_58.59 | all-reduce | flops 8192 | bytes 65536 | tf_op jit(solution)/shard_map/psum | solution.py:265
  345.6 609.3 %all-reduce.4.cloned.1.call-done = (f32[1024,1536]{1,0:T(8,128)}, f32[512,1024]{1,0:T(8,128)}, f32[1024,2048]{1,0:T(8,128)}, f32[2048,1024]{1,0:T(8,128)}) async-done(((f32[1024,1536]{1,0:T(8,128)}, f32[512,1024]{1,0:T(8,128)}, f32[1024,2048]{1,0:T(8,128)}, f32[2048,1024]{1,0:T(8,128)}), (f32[1024,1536]{1,0:T(8,128)}, f32[512,1024]{1,0:T(8,128)}, f32[1024,2048]{1,0:T(8,128)}, ...) | async-done | bytes 25165840 | tf_op jit(solution)/shard_map/psum | solution.py:262
  954.9 6.3 fusion.117
  963.8 4.3 copy.94
  (407 shorter events, 150.0 us)
Async XLA Ops:
  7.2 37.5 %copy-start = (bf16[512,1024]{1,0:T(8,128)(2,1)S(1)}, bf16[512,1024]{1,0:T(8,128)(2,1)}, u32[]{:S(2)}) copy-start(bf16[512,1024]{1,0:T(8,128)(2,1)} %param.22) | copy-start | bytes 3145732
  7.2 18.5 %all-gather.13.cloned.1.call-start = ((), (), s32[]{:S(2)}) async-start(), calls=%async_computation.12 | async-start | bytes 1572864 | tf_op jit(solution)/shard_map/all_gather | solution.py:172
  13.8 33.5 %all-gather.9.cloned.1.call-start = ((), (), s32[]{:S(2)}) async-start(), calls=%async_computation.8 | async-start | bytes 1572864 | tf_op jit(solution)/shard_map/all_gather | solution.py:172
  14.5 52.7 %reduce-scatter.13.cloned.1.call-start = ((), (), s32[]{:S(2)}) async-start(), calls=%async_computation.13 | async-start | bytes 3145728 | tf_op jit(solution)/shard_map/reduce_scatter | solution.py:183
  21.8 35.5 %copy-start.58 = (f32[512,32]{0,1:T(8,128)}, f32[512,32]{0,1:T(8,128)S(1)}, u32[]{:S(2)}) copy-start(f32[512,32]{0,1:T(8,128)S(1)} %get-tuple-element.245) | copy-start | bytes 196612
  21.8 35.5 %copy-start.60 = (f32[512,32]{0,1:T(8,128)}, f32[512,32]{0,1:T(8,128)S(1)}, u32[]{:S(2)}) copy-start(f32[512,32]{0,1:T(8,128)S(1)} %get-tuple-element.246) | copy-start | bytes 196612
  46.8 31.4 %reduce-scatter.9.cloned.1.call-start = ((), (), s32[]{:S(2)}) async-start(), calls=%async_computation.9 | async-start | bytes 3145728 | tf_op jit(solution)/shard_map/reduce_scatter | solution.py:183
  67.2 28.9 %all-gather.15.cloned.1.call-start = ((), (), s32[]{:S(2)}) async-start(), calls=%async_computation.14 | async-start | bytes 1572864 | tf_op jit(solution)/shard_map/all_gather | solution.py:193
  85.7 30.9 %all-gather.11.cloned.1.call-start = ((), (), s32[]{:S(2)}) async-start(), calls=%async_computation.10 | async-start | bytes 1572864 | tf_op jit(solution)/shard_map/all_gather | solution.py:193
  86.3 50.3 %reduce-scatter.15.cloned.1.call-start = ((), (), s32[]{:S(2)}) async-start(), calls=%async_computation.15 | async-start | bytes 3145728 | tf_op jit(solution)/shard_map/reduce_scatter | solution.py:197
  96.1 16.3 %copy-start.97 = (bf16[2048,1024]{1,0:T(8,128)(2,1)S(1)}, bf16[2048,1024]{1,0:T(8,128)(2,1)}, u32[]{:S(2)}) copy-start(bf16[2048,1024]{1,0:T(8,128)(2,1)} %param.24) | copy-start | bytes 12582916
  116.1 31.3 %reduce-scatter.11.cloned.1.call-start = ((), (), s32[]{:S(2)}) async-start(), calls=%async_computation.11 | async-start | bytes 3145728 | tf_op jit(solution)/shard_map/reduce_scatter | solution.py:197
  136.5 16.7 %copy-start.6 = (f32[256,1024]{1,0:T(8,128)S(1)}, f32[256,1024]{1,0:T(8,128)}, u32[]{:S(2)}) copy-start(f32[256,1024]{1,0:T(8,128)} %copy-done.5) | copy-start | bytes 3145732
  136.5 16.7 %copy-start.94 = (f32[1024]{0:T(1024)S(1)}, f32[1024]{0:T(1024)}, u32[]{:S(2)}) copy-start(f32[1024]{0:T(1024)} %param.32) | copy-start | bytes 12292
  136.5 30.1 %all-gather.21.cloned.1.call-start = ((), (), s32[]{:S(2)}) async-start(), calls=%async_computation.20 | async-start | bytes 1572864 | tf_op jit(solution)/shard_map/all_gather | solution.py:208
  156.3 24.0 %all-gather.17.cloned.1.call-start = ((), (), s32[]{:S(2)}) async-start(), calls=%async_computation.16 | async-start | bytes 1572864 | tf_op jit(solution)/shard_map/all_gather | solution.py:208
  158.5 43.2 %reduce-scatter.21.cloned.1.call-start = ((), (), s32[]{:S(2)}) async-start(), calls=%async_computation.21 | async-start | bytes 3145728 | tf_op jit(solution)/shard_map/reduce_scatter | solution.py:214
  180.2 25.8 %reduce-scatter.17.cloned.1.call-start = ((), (), s32[]{:S(2)}) async-start(), calls=%async_computation.17 | async-start | bytes 3145728 | tf_op jit(solution)/shard_map/reduce_scatter | solution.py:214
  193.9 37.0 %all-gather.23.cloned.1.call-start = ((), (), s32[]{:S(2)}) async-start(), calls=%async_computation.22 | async-start | bytes 1572864 | tf_op jit(solution)/shard_map/all_gather | solution.py:220
  214.0 35.5 %all-gather.19.cloned.1.call-start = ((), (), s32[]{:S(2)}) async-start(), calls=%async_computation.18 | async-start | bytes 1572864 | tf_op jit(solution)/shard_map/all_gather | solution.py:220
  230.4 61.7 %reduce-scatter.23.cloned.1.call-start = ((), (), s32[]{:S(2)}) async-start(), calls=%async_computation.23 | async-start | bytes 1572864 | tf_op jit(solution)/shard_map/reduce_scatter | solution.py:239
  249.3 42.8 %reduce-scatter.19.cloned.1.call-start = ((), (), s32[]{:S(2)}) async-start(), calls=%async_computation.19 | async-start | bytes 1572864 | tf_op jit(solution)/shard_map/reduce_scatter | solution.py:239
  268.2 686.7 %all-reduce.4.cloned.1.call-start = ((), (), s32[]{:S(2)}) async-start(), calls=%async_computation.24 | async-start | bytes 50331648 | tf_op jit(solution)/shard_map/psum | solution.py:262
  289.6 52.5 %copy-start.15 = (f32[256,1024]{1,0:T(8,128)S(1)}, f32[256,1024]{1,0:T(8,128)}, u32[]{:S(2)}) copy-start(f32[256,1024]{1,0:T(8,128)} %copy-done.14) | copy-start | bytes 3145732
  (107 other events, 465.9 us)
Sparse Core Ops, SparseCore 0:
  13.9 11.8 all-gather.12
  27.9 10.1 all-gather.8
  46.9 10.6 reduce-scatter.12
  67.3 10.8 reduce-scatter.8
  85.9 10.2 all-gather.14
  98.1 10.1 all-gather.10
  116.2 10.7 reduce-scatter.14
  136.6 10.7 reduce-scatter.10
  156.4 10.2 all-gather.20
  168.6 10.1 all-gather.16
  181.7 10.7 reduce-scatter.20
  195.2 10.7 reduce-scatter.16
  214.2 10.2 all-gather.22
  230.5 10.2 all-gather.18
  249.4 9.7 reduce-scatter.22
  268.3 9.7 reduce-scatter.18
  288.4 666.4 all-reduce.3
where the time goes:
time: 988 us; the launch traced here: 980 us
  waiting for transfers between devices  653 us (66%)
  matrix products  151 us (15%)
  other arithmetic  59.3 us (6%)
  local copies, waits for them, and re-layouts  53.1 us (5%)
  blocking collectives  45.4 us (5%)
  between operations  15.9 us (2%)
    psum x1, waiting for transfers between devices, on_device(): lax.psum((joined_acc, output_acc, inner_acc, outer_acc), 'dp')  609 us
    psum x1, blocking collectives, on_device(): lax.psum((norm_acc[0], norm_acc[1], norm_acc[2], norm_acc[3], norm_acc[4]...  45.4 us
    dot_general x8, matrix products, contract_rows(): lax.dot_general(left, right, (((0,), (0,)), ((), ())), preferred_element_...  41.9 us
    dot_general x8, matrix products, times_transpose(): lax.dot_general(left, right, (((1,), (1,)), ((), ())), preferred_element_...  34 us
    unnamed x233, local copies, waits for them, and re-layouts  32.4 us
    dot_general x2, matrix products, on_device(): pre_act = jnp.dot(feed, inner_use, preferred_element_type=jnp.float32)  29.8 us
  transfers between devices with their start and end apart: 17, of which 7 were waited for; matrix products, arithmetic and copies ran while one was open for 20% of the time, Pallas kernels for 0%

commit v1 on v0

--- a/solution.py
+++ b/solution.py
@@ -22,7 +22,8 @@
 
 
 def seq_layout(lens, rows):
-    ends = jnp.cumsum(lens, dtype=jnp.int32)
+    slot = jnp.arange(lens.shape[0], dtype=jnp.int32)
+    ends = jnp.sum(jnp.where(slot[None, :] <= slot[:, None], lens[None, :], 0), axis=1)
     index = jnp.arange(rows, dtype=jnp.int32)
     after = index[:, None] >= ends[None, :]
     segment = jnp.sum(after.astype(jnp.int32), axis=1)

time: 988 us -> 986 us (level)
  no operation moved by 1% of the time
where the time goes in v1:
time: 986 us; the launch traced here: 978 us
  waiting for transfers between devices  655 us (66%)
  matrix products  151 us (15%)
  other arithmetic  58.1 us (6%)
  local copies, waits for them, and re-layouts  48.9 us (5%)
  blocking collectives  45.5 us (5%)
  between operations  16.2 us (2%)
    psum x1, waiting for transfers between devices, on_device(): lax.psum((joined_acc, output_acc, inner_acc, outer_acc), 'dp')  609 us
    psum x1, blocking collectives, on_device(): lax.psum((norm_acc[0], norm_acc[1], norm_acc[2], norm_acc[3], norm_acc[4]...  45.5 us
    dot_general x8, matrix products, contract_rows(): lax.dot_general(left, right, (((0,), (0,)), ((), ())), preferred_element_...  42.6 us
    dot_general x8, matrix products, times_transpose(): lax.dot_general(left, right, (((1,), (1,)), ((), ())), preferred_element_...  34 us
    unnamed x233, local copies, waits for them, and re-layouts  30.5 us
    dot_general x2, matrix products, on_device(): pre_act = jnp.dot(feed, inner_use, preferred_element_type=jnp.float32)  29.8 us
  transfers between devices with their start and end apart: 17, of which 7 were waited for; matrix products, arithmetic and copies ran while one was open for 20% of the time, Pallas kernels for 0%

profile of v1, /device:TPU:0, one launch (start us, length us, event | category | flops | bytes accessed | tf_op | source)
XLA Modules:
  0.0 977.7 jit_solution(1756419847661336057)
XLA Ops:
  19.0 6.7 all-gather.13.cloned.1.call-done
  25.7 4.0 fusion.125
  46.4 4.0 fusion.122
  68.5 8.1 reduce-scatter.9.cloned.1.call-done
  85.2 9.3 all-gather.15.cloned.1.call-done
  94.5 15.0 %multiply_convert_fusion.2 = (bf16[512,2048]{1,0:T(8,128)(2,1)S(1)}, f32[512,2048]{1,0:T(8,128)}, f32[512,2048]{1,0:T(8,128)}) fusion(bf16[512,1024]{1,0:T(8,128)(2,1)} %all-gather.15.cloned.1.call-done, bf16[1024,2048]{1,0:T(8,128)(2,1)} %param.23), kind=kOutput, calls=%fused_computation.27 | convolution fusion | flops 2215641088 | bytes 15728640 | tf_op jit(solution)/shard_map/dot_general | solution.py:195
  114.8 14.9 %multiply_convert_fusion.3 = (bf16[512,2048]{1,0:T(8,128)(2,1)S(1)}, f32[512,2048]{1,0:T(8,128)}, f32[512,2048]{1,0:T(8,128)}) fusion(bf16[512,1024]{1,0:T(8,128)(2,1)} %all-gather.11.cloned.1.call-done, bf16[1024,2048]{1,0:T(8,128)(2,1)} %param.23), kind=kOutput, calls=%fused_computation.40 | convolution fusion | flops 2215641088 | bytes 15728640 | tf_op jit(solution)/shard_map/dot_general | solution.py:195
  137.7 7.9 reduce-scatter.11.cloned.1.call-done
  156.9 7.9 all-gather.21.cloned.1.call-done
  164.8 8.5 add_convert_fusion
  178.4 8.5 add_convert_fusion.1
  188.3 3.7 fusion.128
  192.5 7.5 fusion.132
  200.0 4.2 reduce-scatter.17.cloned.1.call-done
  211.6 10.1 %convolution_add_fusion.1 = f32[2048,1024]{1,0:T(8,128)} fusion(f32[2048,1024]{1,0:T(8,128)} %fusion.132, bf16[512,2048]{1,0:T(8,128)(2,1)} %copy-done.17, bf16[512,1024]{1,0:T(8,128)(2,1)} %all-gather.21.cloned.1.call-done), kind=kOutput, calls=%fused_computation.57 | convolution fusion | flops 2149580800 | bytes 19922944 | tf_op jit(solution)/shard_map/dot_general | solution.py:60
  221.7 5.7 fusion.131
  230.6 5.4 multiply_reduce_fusion
  249.3 5.4 multiply_reduce_fusion.1
  266.3 9.9 %convolution_add_fusion.2 = f32[1024,2048]{1,0:T(8,128)} fusion(f32[1024,2048]{1,0:T(8,128)} %fusion.131, bf16[512,1024]{1,0:T(8,128)(2,1)S(1)} %copy-done.20, bf16[512,2048]{1,0:T(8,128)(2,1)} %copy-done.21), kind=kOutput, calls=%fused_computation.58 | convolution fusion | flops 2149580800 | bytes 19922944 | tf_op jit(solution)/shard_map/dot_general | solution.py:60
  281.4 4.6 convolution_add_fusion
  294.5 45.5 %all-reduce = (f32[1024]{0:T(1024)}, f32[1024]{0:T(1024)}, f32[1024]{0:T(1024)}, f32[1024]{0:T(1024)}, f32[1024]{0:T(1024)}, /*index=5*/f32[1024]{0:T(1024)}, f32[1024]{0:T(1024)}, f32[1024]{0:T(1024)}) all-reduce(f32[1024]{0:T(1024)S(1)} %add.355, f32[1024]{0:T(1024)S(1)} %add.356, ...), channel_id=1, replica_groups=mesh['dp'=16,'tensor'=2] {'dp','tensor'}, use_global_device_ids=true, to_apply=%region_58.59 | all-reduce | flops 8192 | bytes 65536 | tf_op jit(solution)/shard_map/psum | solution.py:266
  343.5 609.3 %all-reduce.4.cloned.1.call-done = (f32[1024,1536]{1,0:T(8,128)}, f32[512,1024]{1,0:T(8,128)}, f32[1024,2048]{1,0:T(8,128)}, f32[2048,1024]{1,0:T(8,128)}) async-done(((f32[1024,1536]{1,0:T(8,128)}, f32[512,1024]{1,0:T(8,128)}, f32[1024,2048]{1,0:T(8,128)}, f32[2048,1024]{1,0:T(8,128)}), (f32[1024,1536]{1,0:T(8,128)}, f32[512,1024]{1,0:T(8,128)}, f32[1024,2048]{1,0:T(8,128)}, ...) | async-done | bytes 25165840 | tf_op jit(solution)/shard_map/psum | solution.py:263
  952.8 6.3 fusion.117
  961.7 4.3 copy.94
  (407 shorter events, 144.7 us)
Async XLA Ops:
  7.2 36.6 %copy-start = (bf16[512,1024]{1,0:T(8,128)(2,1)S(1)}, bf16[512,1024]{1,0:T(8,128)(2,1)}, u32[]{:S(2)}) copy-start(bf16[512,1024]{1,0:T(8,128)(2,1)} %param.22) | copy-start | bytes 3145732
  7.2 18.4 %all-gather.13.cloned.1.call-start = ((), (), s32[]{:S(2)}) async-start(), calls=%async_computation.12 | async-start | bytes 1572864 | tf_op jit(solution)/shard_map/all_gather | solution.py:173
  13.8 32.6 %all-gather.9.cloned.1.call-start = ((), (), s32[]{:S(2)}) async-start(), calls=%async_computation.8 | async-start | bytes 1572864 | tf_op jit(solution)/shard_map/all_gather | solution.py:173
  14.5 51.1 %reduce-scatter.13.cloned.1.call-start = ((), (), s32[]{:S(2)}) async-start(), calls=%async_computation.13 | async-start | bytes 3145728 | tf_op jit(solution)/shard_map/reduce_scatter | solution.py:184
  18.9 16.7 %copy-start.61 = (f32[512,32]{0,1:T(8,128)}, f32[512,32]{0,1:T(8,128)S(1)}, u32[]{:S(2)}) copy-start(f32[512,32]{0,1:T(8,128)S(1)} %get-tuple-element.251) | copy-start | bytes 196612
  18.9 16.7 %copy-start.63 = (f32[512,32]{0,1:T(8,128)}, f32[512,32]{0,1:T(8,128)S(1)}, u32[]{:S(2)}) copy-start(f32[512,32]{0,1:T(8,128)S(1)} %get-tuple-element.252) | copy-start | bytes 196612
  18.9 37.5 %copy-start.57 = (f32[512,32]{0,1:T(8,128)}, f32[512,32]{0,1:T(8,128)S(1)}, u32[]{:S(2)}) copy-start(f32[512,32]{0,1:T(8,128)S(1)} %get-tuple-element.245) | copy-start | bytes 196612
  18.9 37.5 %copy-start.59 = (f32[512,32]{0,1:T(8,128)}, f32[512,32]{0,1:T(8,128)S(1)}, u32[]{:S(2)}) copy-start(f32[512,32]{0,1:T(8,128)S(1)} %get-tuple-element.246) | copy-start | bytes 196612
  45.9 30.7 %reduce-scatter.9.cloned.1.call-start = ((), (), s32[]{:S(2)}) async-start(), calls=%async_computation.9 | async-start | bytes 3145728 | tf_op jit(solution)/shard_map/reduce_scatter | solution.py:184
  65.5 29.0 %all-gather.15.cloned.1.call-start = ((), (), s32[]{:S(2)}) async-start(), calls=%async_computation.14 | async-start | bytes 1572864 | tf_op jit(solution)/shard_map/all_gather | solution.py:194
  84.1 30.6 %all-gather.11.cloned.1.call-start = ((), (), s32[]{:S(2)}) async-start(), calls=%async_computation.10 | async-start | bytes 1572864 | tf_op jit(solution)/shard_map/all_gather | solution.py:194
  84.7 50.0 %reduce-scatter.15.cloned.1.call-start = ((), (), s32[]{:S(2)}) async-start(), calls=%async_computation.15 | async-start | bytes 3145728 | tf_op jit(solution)/shard_map/reduce_scatter | solution.py:198
  114.5 31.0 %reduce-scatter.11.cloned.1.call-start = ((), (), s32[]{:S(2)}) async-start(), calls=%async_computation.11 | async-start | bytes 3145728 | tf_op jit(solution)/shard_map/reduce_scatter | solution.py:198
  134.6 16.7 %copy-start.6 = (f32[256,1024]{1,0:T(8,128)S(1)}, f32[256,1024]{1,0:T(8,128)}, u32[]{:S(2)}) copy-start(f32[256,1024]{1,0:T(8,128)} %copy-done.5) | copy-start | bytes 3145732
  134.7 30.1 %all-gather.21.cloned.1.call-start = ((), (), s32[]{:S(2)}) async-start(), calls=%async_computation.20 | async-start | bytes 1572864 | tf_op jit(solution)/shard_map/all_gather | solution.py:209
  154.4 24.0 %all-gather.17.cloned.1.call-start = ((), (), s32[]{:S(2)}) async-start(), calls=%async_computation.16 | async-start | bytes 1572864 | tf_op jit(solution)/shard_map/all_gather | solution.py:209
  156.6 43.4 %reduce-scatter.21.cloned.1.call-start = ((), (), s32[]{:S(2)}) async-start(), calls=%async_computation.21 | async-start | bytes 3145728 | tf_op jit(solution)/shard_map/reduce_scatter | solution.py:215
  178.3 25.8 %reduce-scatter.17.cloned.1.call-start = ((), (), s32[]{:S(2)}) async-start(), calls=%async_computation.17 | async-start | bytes 3145728 | tf_op jit(solution)/shard_map/reduce_scatter | solution.py:215
  192.0 36.6 %all-gather.23.cloned.1.call-start = ((), (), s32[]{:S(2)}) async-start(), calls=%async_computation.22 | async-start | bytes 1572864 | tf_op jit(solution)/shard_map/all_gather | solution.py:221
  211.5 35.9 %all-gather.19.cloned.1.call-start = ((), (), s32[]{:S(2)}) async-start(), calls=%async_computation.18 | async-start | bytes 1572864 | tf_op jit(solution)/shard_map/all_gather | solution.py:221
  228.4 61.5 %reduce-scatter.23.cloned.1.call-start = ((), (), s32[]{:S(2)}) async-start(), calls=%async_computation.23 | async-start | bytes 1572864 | tf_op jit(solution)/shard_map/reduce_scatter | solution.py:240
  247.1 42.9 %reduce-scatter.19.cloned.1.call-start = ((), (), s32[]{:S(2)}) async-start(), calls=%async_computation.19 | async-start | bytes 1572864 | tf_op jit(solution)/shard_map/reduce_scatter | solution.py:240
  265.9 686.9 %all-reduce.4.cloned.1.call-start = ((), (), s32[]{:S(2)}) async-start(), calls=%async_computation.24 | async-start | bytes 50331648 | tf_op jit(solution)/shard_map/psum | solution.py:263
  287.5 52.5 %copy-start.15 = (f32[256,1024]{1,0:T(8,128)S(1)}, f32[256,1024]{1,0:T(8,128)}, u32[]{:S(2)}) copy-start(f32[256,1024]{1,0:T(8,128)} %copy-done.14) | copy-start | bytes 3145732
  (107 other events, 481.0 us)
Sparse Core Ops, SparseCore 0:
  13.9 11.7 all-gather.12
  27.8 10.1 all-gather.8
  46.0 10.7 reduce-scatter.12
  65.7 10.8 reduce-scatter.8
  84.3 10.1 all-gather.14
  96.5 10.1 all-gather.10
  114.6 10.7 reduce-scatter.14
  134.8 10.7 reduce-scatter.10
  154.5 10.2 all-gather.20
  166.7 10.1 all-gather.16
  179.8 10.7 reduce-scatter.20
  193.4 10.7 reduce-scatter.16
  211.6 10.2 all-gather.22
  228.5 10.2 all-gather.18
  247.2 9.6 reduce-scatter.22
  266.0 9.6 reduce-scatter.18
  286.2 666.5 all-reduce.3
